TPU v7x, 512 devices: a whole 4x8x8 slice. The times are simulated.
512 devices in a mesh: section: 8 (over x, core), fsdp: 32 (over y_lo, z), tile: 2 (over y_hi).
Axes of the slice: x: 4, y: 8 (y_hi: 2, y_lo: 4; y = y_hi * 4 + y_lo), z: 8, core: 2. Of those that a mesh axis runs over, the one named last changes fastest.
Arguments:
- features: bfloat16 [4, 8192, 320], P(None, ('fsdp', 'tile')), may hold values from -6 to 6
- labels: int32 [4, 8192], P(None, ('fsdp', 'tile')), may hold values from 0 to 4
- w_expand: bfloat16 [8, 320, 1280], P('section', None, 'fsdp'), may hold values from -0.3125 to 0.3125
- w_reduce: bfloat16 [8, 320, 1280], P('section', None, 'fsdp'), may hold values from -0.15625 to 0.15625
- head_weight: bfloat16 [320, 5], replicated, may hold values from -0.3125 to 0.3125
Outputs:
- grad_expand: float32 [8, 320, 1280], P('section', None, 'fsdp')
- grad_reduce: float32 [8, 320, 1280], P('section', None, 'fsdp')
All inputs are finite; a program needn't handle non-finite values.
Results may differ from a plain program's by a relative error of at most 0.01.
Values may be sent and summed in bfloat16 or wider, within the bound.
A program may use at most 64 MiB of HBM per device.

v0:
```python
import math

import jax
import jax.numpy as jnp
from jax import lax
from jax.sharding import PartitionSpec as P

norm_eps = 1e-06


def from_behind(value, axis, steps):
    count = lax.axis_size(axis)
    leading, last = (max(0, -steps), min(count, count - steps))
    return lax.ppermute(value, axis, [(source, source + steps) for source in range(leading, last)])


def normalize(values):
    floats = values.astype(jnp.float32)
    centred = floats - jnp.mean(floats, axis=-1, keepdims=True)
    inverse_std = lax.rsqrt(jnp.mean(centred * centred, axis=-1, keepdims=True) + norm_eps)
    return (centred * inverse_std, inverse_std)


def norm_back(values, grad_norm):
    unit, inverse_std = normalize(values)
    centred_grad = grad_norm - jnp.mean(grad_norm, axis=-1, keepdims=True)
    return inverse_std * (centred_grad - unit * jnp.mean(grad_norm * unit, axis=-1, keepdims=True))


def section_forward(inputs, w_up, w_down):
    unit, _ = normalize(inputs)
    normed = unit.astype(jnp.bfloat16)
    hidden_pre = jnp.dot(normed, w_up, preferred_element_type=jnp.float32)
    hidden = jax.nn.gelu(hidden_pre).astype(jnp.bfloat16)
    branch = lax.dot_general(
        hidden, w_down, (((1,), (1,)), ((), ())), preferred_element_type=jnp.float32
    )
    return ((inputs.astype(jnp.float32) + branch).astype(jnp.bfloat16), hidden_pre)


def section_backward(inputs, hidden_pre, grad_out, w_up, w_down):
    unit, _ = normalize(inputs)
    normed = unit.astype(jnp.bfloat16)
    hidden = jax.nn.gelu(hidden_pre).astype(jnp.bfloat16)
    grad_down = lax.dot_general(
        grad_out, hidden, (((0,), (0,)), ((), ())), preferred_element_type=jnp.float32
    )
    grad_hidden = jnp.dot(grad_out, w_down, preferred_element_type=jnp.float32)
    grad_pre = jax.vjp(jax.nn.gelu, hidden_pre)[1](grad_hidden)[0].astype(jnp.bfloat16)
    grad_up = lax.dot_general(
        normed, grad_pre, (((0,), (0,)), ((), ())), preferred_element_type=jnp.float32
    )
    grad_norm = lax.dot_general(
        grad_pre, w_up, (((1,), (1,)), ((), ())), preferred_element_type=jnp.float32
    )
    grad_in = (grad_out.astype(jnp.float32) + norm_back(inputs, grad_norm)).astype(jnp.bfloat16)
    return (grad_up, grad_down, grad_in)


def head_backward(outputs, pixel_labels, head_weight, loss_scale):
    unit, _ = normalize(outputs)
    normed = unit.astype(jnp.bfloat16)
    logits = jnp.dot(normed, head_weight, preferred_element_type=jnp.float32)
    exponent = jnp.exp(logits)
    probs = exponent / jnp.sum(exponent, axis=-1, keepdims=True)
    classes = lax.broadcasted_iota(jnp.int32, logits.shape, 1)
    onehot = (classes == pixel_labels[:, None]).astype(jnp.float32)
    grad_logits = ((probs - onehot) * loss_scale).astype(jnp.bfloat16)
    grad_norm = lax.dot_general(
        grad_logits, head_weight, (((1,), (1,)), ((), ())), preferred_element_type=jnp.float32
    )
    return norm_back(outputs, grad_norm).astype(jnp.bfloat16)


def keep_slot(buffer, value, slot, flag):
    previous = lax.dynamic_index_in_dim(buffer, slot, 0, keepdims=False)
    updated = jnp.where(flag, value, previous)
    return lax.dynamic_update_index_in_dim(buffer, updated, slot, 0)


def local(features, labels, w_expand, w_reduce, head_weight):
    section_count = lax.axis_size("section")
    section_index = lax.axis_index("section")
    micro_count, row_count, feat_width = features.shape
    loss_scale = 1.0 / math.sqrt(
        micro_count * row_count * lax.axis_size("fsdp") * lax.axis_size("tile")
    )
    w_up, w_down = (
        lax.all_gather(w_expand[0], "fsdp", axis=1, tiled=True),
        lax.all_gather(w_reduce[0], "fsdp", axis=1, tiled=True),
    )
    hidden_width = w_up.shape[1]
    tick_count = micro_count + section_count - 1
    ticks_all = jnp.arange(tick_count, dtype=jnp.int32)
    is_first = section_index == 0
    is_last = section_index == section_count - 1

    def forward_tick(state_carry, tick_number):
        incoming, saved_inputs, saved_pre, saved_grads = state_carry
        micro_index = tick_number - section_index
        is_valid = (micro_index >= 0) & (micro_index < micro_count)
        slot = jnp.clip(micro_index, 0, micro_count - 1)
        own_rows = lax.dynamic_index_in_dim(features, slot, 0, keepdims=False)
        inputs = jnp.where(is_first, own_rows, incoming)
        outputs, hidden_pre = section_forward(inputs, w_up, w_down)
        own_labels = lax.dynamic_index_in_dim(labels, slot, 0, keepdims=False)
        head_grad = head_backward(outputs, own_labels, head_weight, loss_scale)
        saved_inputs = keep_slot(saved_inputs, inputs, slot, is_valid)
        saved_pre = keep_slot(saved_pre, hidden_pre, slot, is_valid)
        saved_grads = keep_slot(saved_grads, head_grad, slot, is_valid & is_last)
        incoming = from_behind(outputs, "section", 1)
        return ((incoming, saved_inputs, saved_pre, saved_grads), None)

    start_rows = jnp.zeros((row_count, feat_width), jnp.bfloat16)
    start_inputs = jnp.zeros((micro_count, row_count, feat_width), jnp.bfloat16)
    start_pre = jnp.zeros((micro_count, row_count, hidden_width), jnp.float32)
    forward_state, _ = lax.scan(
        forward_tick, (start_rows, start_inputs, start_pre, start_inputs), ticks_all
    )
    _, saved_inputs, saved_pre, saved_grads = forward_state
    up_back, down_back = (
        lax.all_gather(w_expand[0], "fsdp", axis=1, tiled=True),
        lax.all_gather(w_reduce[0], "fsdp", axis=1, tiled=True),
    )

    def backward_tick(state_carry, tick_number):
        incoming, up_total, down_total = state_carry
        micro_index = tick_number - (section_count - 1 - section_index)
        is_valid = (micro_index >= 0) & (micro_index < micro_count)
        slot = jnp.clip(micro_index, 0, micro_count - 1)
        last_grad = lax.dynamic_index_in_dim(saved_grads, slot, 0, keepdims=False)
        grad_out = jnp.where(is_last, last_grad, incoming)
        inputs = lax.dynamic_index_in_dim(saved_inputs, slot, 0, keepdims=False)
        hidden_pre = lax.dynamic_index_in_dim(saved_pre, slot, 0, keepdims=False)
        grad_up, grad_down, grad_in = section_backward(
            inputs, hidden_pre, grad_out, up_back, down_back
        )
        up_total = up_total + jnp.where(is_valid, grad_up, 0.0)
        down_total = down_total + jnp.where(is_valid, grad_down, 0.0)
        incoming = from_behind(grad_in, "section", -1)
        return ((incoming, up_total, down_total), None)

    zero_grads = jnp.zeros((feat_width, hidden_width), jnp.float32)
    backward_state, _ = lax.scan(backward_tick, (start_rows, zero_grads, zero_grads), ticks_all)
    _, up_total, down_total = backward_state
    up_shard, down_shard = (
        lax.psum_scatter(up_total, "fsdp", scatter_dimension=1, tiled=True),
        lax.psum_scatter(down_total, "fsdp", scatter_dimension=1, tiled=True),
    )
    up_shard, down_shard = lax.psum((up_shard, down_shard), "tile")
    return (up_shard[None], down_shard[None])


def solution(mesh):
    return jax.shard_map(
        local,
        mesh=mesh,
        in_specs=(
            P(None, ("fsdp", "tile"), None),
            P(None, ("fsdp", "tile")),
            P("section", None, "fsdp"),
            P("section", None, "fsdp"),
            P(),
        ),
        out_specs=(P("section", None, "fsdp"), P("section", None, "fsdp")),
        check_vma=False,
    )
```

profile of v0, /device:TPU:1, one launch (start us, length us, event | category | flops | bytes accessed | tf_op | source)
XLA Modules:
  0.0 798.2 jit_solution(8618754317241825508)
XLA Ops:
  7.2 77.4 %all-gather = bf16[1,320,1280]{1,2,0:T(8,128)(2,1)S(1)} all-gather(bf16[1,320,40]{1,2,0:T(8,128)(2,1)} %param.11), channel_id=2, replica_groups=mesh['section'=8,'fsdp'=32,'tile'=2] {'fsdp'}, dimensions={2}, use_global_device_ids=true | all-gather | bytes 844800 | tf_op jit(solution)/shard_map/all_gather | solution.py:89
  85.3 64.9 %all-gather.1 = bf16[1,320,1280]{1,2,0:T(8,128)(2,1)S(1)} all-gather(bf16[1,320,40]{1,2,0:T(8,128)(2,1)S(1)} %copy-done.1), channel_id=3, replica_groups=mesh['section'=8,'fsdp'=32,'tile'=2] {'fsdp'}, dimensions={2}, use_global_device_ids=true | all-gather | bytes 844800 | tf_op jit(solution)/shard_map/all_gather | solution.py:90
  153.4 146.3 %while.33 = (s32[]{:T(128)}, bf16[128,320]{0,1:T(8,128)(2,1)S(1)}, bf16[4,128,320]{1,2,0:T(8,128)(2,1)S(1)}, f32[4,128,1280]{2,1,0:T(8,128)}, bf16[4,128,320]{1,...) while((s32[]{:T(128)}, bf16[128,320]{0,1:T(8,128)(2,1)S(1)}, ...), condition=%wide.region_8.9_spmd, body=%wide.region_0.8_spmd.sunk | while | flops 213815808 | bytes 11170897 | solution.py:117
  158.5 30.9 %collective-permute-start = (bf16[128,320]{0,1:T(8,128)(2,1)S(1)}, bf16[128,320]{0,1:T(8,128)(2,1)S(1)}, u32[]{:S(2)}, u32[]{:S(2)}) collective-permute-start(bf16[128,320]{0,1:T(8,128)(2,1)S(1)} %get-tuple-element.536), channel_id=1, source_target_pairs={{0,64},{64,128},{128,192},{192,256},{256,320},{320,384},{384,448},... | collective-permute-start | bytes 245768 | tf_op jit(solution)/shard_map/while/body/eval_jaxpr/ppermute | solution.py:14
  196.0 4.3 collective-permute-start
  206.9 4.3 collective-permute-start
  217.8 4.3 collective-permute-start
  228.7 4.3 collective-permute-start
  239.6 4.3 collective-permute-start
  250.4 4.3 collective-permute-start
  261.3 4.3 collective-permute-start
  272.2 4.3 collective-permute-start
  283.1 4.3 collective-permute-start
  293.9 4.3 collective-permute-start
  300.3 126.7 %while.34 = (s32[]{:T(128)}, bf16[128,320]{0,1:T(8,128)(2,1)}, f32[320,1280]{1,0:T(8,128)S(1)}, f32[320,1280]{1,0:T(8,128)}, pred[]{:T(512)}, /*index=5*/s32[11]...) while((s32[]{:T(128)}, bf16[128,320]{0,1:T(8,128)(2,1)}, ...), condition=%wide.region_14.15_spmd.clone, body=%wide.region_9.0_spmd.clone.sunk | while | flops 427745408 | bytes 12135216 | solution.py:144
  331.7 3.3 fusion.147
  343.2 3.3 fusion.147
  354.7 3.3 fusion.147
  389.1 3.3 fusion.147
  400.5 3.3 fusion.147
  412.0 3.3 fusion.147
  431.8 132.8 %reduce-scatter.9.cloned.1.call-done = f32[320,40]{0,1:T(8,128)} async-done(((f32[320,1280]{0,1:T(8,128)}), f32[320,40]{0,1:T(8,128)}) %reduce-scatter.9.cloned.1.call-update) | async-done | bytes 51216
  564.6 160.6 %reduce-scatter.11.cloned.1.call-done = f32[320,40]{0,1:T(8,128)} async-done(((f32[320,1280]{0,1:T(8,128)}), f32[320,40]{0,1:T(8,128)}) %reduce-scatter.11.cloned.1.call-update) | async-done | bytes 51216
  725.2 63.6 %all-reduce.5.cloned.1.call-done = (f32[1,320,40]{1,2,0:T(8,128)}, f32[1,320,40]{1,2,0:T(8,128)}) async-done(((f32[1,320,40]{1,2,0:T(8,128)}, f32[1,320,40]{1,2,0:T(8,128)}), (f32[1,320,40]{1,2,0:T(8,128)}, f32[1,320,40]{1,2,0:T(8,128)})) %all-reduce.5.cloned.1.call-update) | async-done | bytes 102416 | tf_op jit(solution)/shard_map/psum | solution.py:150
  (415 shorter events, 176.8 us)
Async XLA Ops:
  7.2 557.5 %reduce-scatter.9.cloned.1.call-start = ((), (), s32[]{:S(2)}) async-start(), calls=%async_computation.2 | async-start | bytes 2027520
  158.5 32.4 %collective-permute-start = (bf16[128,320]{0,1:T(8,128)(2,1)S(1)}, bf16[128,320]{0,1:T(8,128)(2,1)S(1)}, u32[]{:S(2)}, u32[]{:S(2)}) collective-permute-start(bf16[128,320]{0,1:T(8,128)(2,1)S(1)} %get-tuple-element.536), channel_id=1, source_target_pairs={{0,64},{64,128},{128,192},{192,256},{256,320},{320,384},{384,448},... | collective-permute-start | bytes 245768 | tf_op jit(solution)/shard_map/while/body/eval_jaxpr/ppermute | solution.py:14
  196.0 5.8 collective-permute-start
  217.8 5.7 collective-permute-start
  228.7 5.8 collective-permute-start
  239.6 5.8 collective-permute-start
  250.4 5.8 collective-permute-start
  261.3 5.8 collective-permute-start
  272.2 5.8 collective-permute-start
  283.1 5.8 collective-permute-start
  293.9 5.8 collective-permute-start
  305.7 6.7 collective-permute-start.1
  317.8 6.1 collective-permute-start.1
  329.3 6.1 collective-permute-start.1
  340.8 6.1 collective-permute-start.1
  352.2 6.1 collective-permute-start.1
  363.7 6.1 collective-permute-start.1
  375.1 6.1 collective-permute-start.1
  386.6 6.1 collective-permute-start.1
  398.1 6.1 collective-permute-start.1
  409.5 6.1 collective-permute-start.1
  421.0 6.1 collective-permute-start.1
  428.9 296.3 %reduce-scatter.11.cloned.1.call-start = ((), (), s32[]{:S(2)}) async-start(), calls=%async_computation.3 | async-start | bytes 2027520
  431.7 357.0 %all-reduce.5.cloned.1.call-start = ((), (), s32[]{:S(2)}) async-start(), calls=%async_computation.4 | async-start | bytes 245760 | tf_op jit(solution)/shard_map/psum | solution.py:150
  (14 other events, 99.3 us)
Sparse Core Ops, SparseCore 0:
  429.0 135.5 reduce-scatter.8
  567.7 157.4 reduce-scatter.10
  728.1 60.6 all-reduce.4
where the time goes:
time: 802 us; the launch traced here: 798 us
  waiting for transfers between devices  363 us (45%)
  blocking collectives  142 us (18%)
  starting transfers between devices  94.9 us (12%)
  matrix products  90.7 us (11%)
  local copies, waits for them, and re-layouts  45 us (6%)
  other arithmetic  33.2 us (4%)
  loops' own time  14.7 us (2%)
  between operations  13.8 us (2%)
    unnamed x5, waiting for transfers between devices  293 us
    ppermute x22, starting transfers between devices, from_behind(): lax.ppermute(value, axis, [(source, source + steps) for source in range(l...  94.8 us
    all_gather x1, blocking collectives, local(): lax.all_gather(w_expand[0], 'fsdp', axis=1, tiled=True)  77.4 us
    all_gather x1, blocking collectives, local(): lax.all_gather(w_reduce[0], 'fsdp', axis=1, tiled=True)  64.9 us
    psum x1, waiting for transfers between devices, local(): up_shard, down_shard = lax.psum((up_shard, down_shard), 'tile')  63.6 us
    dot_general x11, matrix products, section_backward(): lax.dot_general(grad_out, hidden, (((0,), (0,)), ((), ())), preferred_ele...  35.7 us
    dot_general x11, matrix products, section_backward(): grad_hidden = jnp.dot(grad_out, w_down, preferred_element_type=jnp.float32)  21.9 us
  transfers between devices with their start and end apart: 25, of which 25 were waited for; matrix products, arithmetic and copies ran while one was open for 7% of the time, Pallas kernels for 0%

commit v1 on v0

v1 whole, which is shorter than its diff:
```python
import math

import jax
import jax.numpy as jnp
from jax import lax
from jax.experimental import pallas as pl
from jax.experimental.pallas import tpu as pltpu
from jax.sharding import PartitionSpec as P

norm_eps = 1e-06
RING = 8
LANES = 128
PACK = 208
HALF = 112
GELU_C = math.sqrt(2.0 / math.pi)
GELU_A = 0.044715
bf16 = jnp.bfloat16
f32 = jnp.float32


def nt(lhs, rhs):
    return lax.dot_general(lhs, rhs, (((1,), (1,)), ((), ())), preferred_element_type=f32)


def nn(lhs, rhs):
    return jnp.dot(lhs, rhs, preferred_element_type=f32)


def tn(lhs, rhs):
    return lax.dot_general(lhs, rhs, (((0,), (0,)), ((), ())), preferred_element_type=f32)


def eye(size):
    row = lax.broadcasted_iota(jnp.int32, (size, size), 0)
    column = lax.broadcasted_iota(jnp.int32, (size, size), 1)
    return jnp.where(row == column, 1.0, 0.0).astype(bf16)


def normalize(values):
    floats = values.astype(f32)
    centred = floats - jnp.mean(floats, axis=0, keepdims=True)
    inverse_std = lax.rsqrt(jnp.mean(centred * centred, axis=0, keepdims=True) + norm_eps)
    return centred * inverse_std, inverse_std


def norm_back(unit, inverse_std, grad):
    centred = grad - jnp.mean(grad, axis=0, keepdims=True)
    return inverse_std * (centred - unit * jnp.mean(grad * unit, axis=0, keepdims=True))


def low_pad(rows):
    return jnp.concatenate([rows, jnp.zeros_like(rows)], axis=0)


def high_pad(rows):
    return jnp.concatenate([jnp.zeros_like(rows), rows], axis=0)


def remote(src, dst, send_sem, recv_sem, device):
    return pltpu.make_async_remote_copy(
        src_ref=src,
        dst_ref=dst,
        send_sem=send_sem,
        recv_sem=recv_sem,
        device_id=device,
        device_id_type=pl.DeviceIdType.MESH,
    )


def kernel(
    sections, groups, tiles, micro, loss_scale,
    feat, labels, wup, wdown, head,
    up_out, down_out,
    gathered, up_t, down_t, mix_t, up_n, down_n, head_pad,
    xbuf, obuf, nbuf, ubuf, istd, pre, hid, gpre, dybuf, dsend,
    parts, ry, rh, qbuf, rz, tbuf, rt,
    gy_s, gz_s, g_r, fs, fr, bs, br, rys, ryr, rhs_, rhr, rzs, rzr, ts, tr,
):
    s = lax.axis_index("section")
    f = lax.axis_index("fsdp")
    t = lax.axis_index("tile")
    y_low, z = f // RING, f % RING
    height = groups * tiles
    y = t * groups + y_low
    last = sections - 1
    block = 40 * RING

    def at(y_new, z_new):
        y_new = (y_new + 2 * height) % height
        z_new = (z_new + 2 * RING) % RING
        return {"fsdp": (y_new % groups) * RING + z_new, "tile": y_new // groups}

    barrier = pltpu.get_barrier_semaphore()
    partners = [at(y, z + d) for d in range(1, RING)]
    if groups == 4:
        partners += [at(y + d, z) for d in (1, -1, 2, -2)]
    if tiles == 2:
        partners.append(at(y + groups, z))
    for device in partners:
        pl.semaphore_signal(barrier, inc=1, device_id=device, device_id_type=pl.DeviceIdType.MESH)

    @pl.when(s > 0)
    def _():
        pl.semaphore_signal(
            barrier, inc=1, device_id={"section": s - 1}, device_id_type=pl.DeviceIdType.MESH
        )

    @pl.when(s < last)
    def _():
        pl.semaphore_signal(
            barrier, inc=1, device_id={"section": s + 1}, device_id_type=pl.DeviceIdType.MESH
        )

    up_w, down_w = wup[0], wdown[0]
    stacked = jnp.concatenate([up_w[:256], down_w[:256], up_w[256:], down_w[256:]], axis=0)
    own = nt(eye(40), stacked)
    pieces = [own[:, LANES * i : LANES * (i + 1)] for i in range(5)]
    pieces.append(jnp.zeros((8, LANES), f32))
    gathered[f] = jnp.concatenate(pieces, axis=0).astype(bf16)

    pl.semaphore_wait(
        barrier,
        len(partners) + jnp.where(s > 0, 1, 0) + jnp.where(s < last, 1, 0),
    )

    def slot(j, dz):
        return ((y_low + j) % groups) * RING + (z + dz + 2 * RING) % RING

    order = (0, 1, 3, 2) if groups == 4 else (0,)
    pending = []
    if groups == 4:
        ysends = [
            remote(gathered.at[f], gathered.at[f], gy_s.at[0], g_r.at[f, 0], at(y + 1, z)),
            remote(gathered.at[f], gathered.at[f], gy_s.at[1], g_r.at[f, 0], at(y - 1, z)),
            remote(
                gathered.at[f, pl.ds(0, HALF)], gathered.at[f, pl.ds(0, HALF)],
                gy_s.at[2], g_r.at[f, 0], at(y + 2, z),
            ),
            remote(
                gathered.at[f, pl.ds(HALF, PACK - HALF)], gathered.at[f, pl.ds(HALF, PACK - HALF)],
                gy_s.at[3], g_r.at[f, 1], at(y - 2, z),
            ),
        ]
        for copy in ysends:
            copy.start()
        pending += ysends

    def arrived(index):
        remote(
            gathered.at[index], gathered.at[index], gy_s.at[0], g_r.at[index, 0], at(y, z + 1)
        ).wait_recv()

    def ysend_arrived(index):
        remote(
            gathered.at[index, pl.ds(0, HALF)], gathered.at[index, pl.ds(0, HALF)],
            gy_s.at[2], g_r.at[index, 0], at(y, z + 1),
        ).wait_recv()
        remote(
            gathered.at[index, pl.ds(HALF, PACK - HALF)], gathered.at[index, pl.ds(HALF, PACK - HALF)],
            gy_s.at[3], g_r.at[index, 1], at(y, z + 1),
        ).wait_recv()

    far = RING // 2
    count = 0
    for step in range(1, far + 1):
        for place, j in enumerate(order):
            if step == 1:
                if j == 2:
                    ysend_arrived(slot(j, 0))
                elif j:
                    arrived(slot(j, 0))
            early = place < (len(order) + 1) // 2
            for side in (1, -1):
                index = slot(j, -side * (step - 1))
                if step > 1:
                    arrived(index)
                if step == far and early != (side == 1):
                    continue
                copy = remote(
                    gathered.at[index], gathered.at[index],
                    gz_s.at[count], g_r.at[index, 0], at(y, z + side),
                )
                copy.start()
                pending.append(copy)
                count += 1
    for j in order:
        arrived(slot(j, far))

    def unpack(pair, carry):
        first = gathered[2 * pair].astype(f32)
        second = gathered[2 * pair + 1].astype(f32)
        rows = pl.ds(pl.multiple_of(pair * 80, 16), 80)

        def both(i):
            return jnp.concatenate(
                [first[40 * i : 40 * i + 40], second[40 * i : 40 * i + 40]], axis=0
            ).astype(bf16)

        up_t[rows, 0:128] = both(0)
        up_t[rows, 128:256] = both(1)
        down_t[rows, 0:128] = both(2)
        down_t[rows, 128:256] = both(3)
        mix_t[rows, :] = both(4)
        return carry

    lax.fori_loop(0, groups * RING // 2, unpack, 0)
    wide = eye(256)
    down_n[0:256, :] = nt(wide, down_t[...]).astype(bf16)
    turned = nt(eye(128), mix_t[...]).astype(bf16)
    down_n[256:320, :] = turned[64:128]

    @pl.when(s > 0)
    def _():
        up_n[0:256, :] = nt(wide, up_t[...]).astype(bf16)
        up_n[256:320, :] = turned[0:64]

    @pl.when(s == 0)
    def _():
        for m in range(micro):
            xbuf[m] = nt(eye(320), feat[m]).astype(bf16)

    @pl.when(s == last)
    def _():
        head_pad[...] = jnp.zeros_like(head_pad)
        head_pad[:, 0:5] = head[...]

    def forward(m, carry):
        @pl.when(s > 0)
        def _():
            remote(obuf.at[m], xbuf.at[m], fs.at[m], fr.at[m], {"section": s}).wait_recv()

        x = xbuf[m]
        unit, inverse_std = normalize(x)
        normed = unit.astype(bf16)
        ubuf[m] = unit
        istd[m] = inverse_std
        nbuf[m] = normed
        low, high = normed[:256], low_pad(normed[256:])
        total = x.astype(f32)
        for g in range(groups):
            rows = slice(block * g, block * (g + 1))
            before = nn(up_t[rows, :], low) + nn(mix_t[rows, :], high)
            pre[m, rows, :] = before
            bent = jnp.tanh(GELU_C * (before + GELU_A * (before * before * before)))
            hidden = (before * (0.5 * (1.0 + bent))).astype(bf16)
            hid[m, rows, :] = hidden
        out = (total + nn(down_n[...], hid[m])).astype(bf16)
        obuf[m] = out

        @pl.when(s < last)
        def _():
            remote(obuf.at[m], xbuf.at[m], fs.at[m], fr.at[m], {"section": s + 1}).start()

        @pl.when(s == last)
        def _():
            head_unit, head_istd = normalize(obuf[m])
            logits = tn(head_pad[...], head_unit.astype(bf16))[0:8]
            classes = lax.broadcasted_iota(jnp.int32, logits.shape, 0)
            exponent = jnp.where(classes < 5, jnp.exp(logits), 0.0)
            probs = exponent / jnp.sum(exponent, axis=0, keepdims=True)
            onehot = jnp.where(classes == labels[pl.ds(m, 1), :], 1.0, 0.0)
            grad_logits = (probs - onehot) * loss_scale
            grad_logits = jnp.concatenate(
                [grad_logits, jnp.zeros((LANES - 8, LANES), f32)], axis=0
            ).astype(bf16)
            grad_norm = nn(head_pad[...], grad_logits)
            dybuf[m] = norm_back(head_unit, head_istd, grad_norm).astype(bf16)

        return carry

    lax.fori_loop(0, micro, forward, 0)

    def backward(m, carry):
        @pl.when(s < last)
        def _():
            remote(dsend.at[m], dybuf.at[m], bs.at[m], br.at[m], {"section": s}).wait_recv()

        dy = dybuf[m]
        low, high = dy[:256], high_pad(dy[256:])
        for g in range(groups):
            rows = slice(block * g, block * (g + 1))
            grad_hidden = nn(down_t[rows, :], low) + nn(mix_t[rows, :], high)
            before = pre[m, rows, :]
            square = before * before
            bent = jnp.tanh(GELU_C * (before + GELU_A * (square * before)))
            slope = 0.5 * (1.0 + bent) + (0.5 * before) * (1.0 - bent * bent) * (
                GELU_C * (1.0 + (3.0 * GELU_A) * square)
            )
            gpre[m, rows, :] = (grad_hidden * slope).astype(bf16)

        @pl.when(s > 0)
        def _():
            grad_norm = nn(up_n[...], gpre[m])
            grad_in = dybuf[m].astype(f32) + norm_back(ubuf[m], istd[m], grad_norm)
            dsend[m] = grad_in.astype(bf16)
            remote(dsend.at[m], dybuf.at[m], bs.at[m], br.at[m], {"section": s - 1}).start()

        return carry

    lax.fori_loop(0, micro, backward, 0)

    normed = jnp.concatenate([nbuf[m] for m in range(micro)], axis=1)
    grads = jnp.concatenate([dybuf[m] for m in range(micro)], axis=1)
    normed_low, normed_high = normed[:256], low_pad(normed[256:])
    grads_low, grads_high = grads[:256], high_pad(grads[256:])

    def weight_grads(g):
        rows = pl.ds(pl.multiple_of(g * block, 16), block)
        grad_pre = jnp.concatenate([gpre[m, rows, :] for m in range(micro)], axis=1)
        hidden = jnp.concatenate([hid[m, rows, :] for m in range(micro)], axis=1)
        up = nt(grad_pre, normed_low)
        down = nt(hidden, grads_low)
        mix = nt(grad_pre, normed_high) + nt(hidden, grads_high)
        for k in range(RING):
            r = slice(40 * k, 40 * k + 40)
            parts[g, k] = jnp.concatenate(
                [up[r, :128], up[r, 128:], down[r, :128], down[r, 128:], mix[r],
                 jnp.zeros((8, LANES), f32)], axis=0,
            ).astype(bf16)

    half = RING // 2
    rsends = []
    if groups == 4:
        g = (y_low + 2) % groups
        weight_grads(g)
        rsends += [
            remote(parts.at[g, pl.ds(0, half)], rh.at[0], rhs_.at[0], rhr.at[0], at(y - 2, z)),
            remote(parts.at[g, pl.ds(half, half)], rh.at[1], rhs_.at[1], rhr.at[1], at(y + 2, z)),
        ]
        rsends[0].start()
        rsends[1].start()
        for i, d in enumerate((1, -1)):
            g = (y_low + d + groups) % groups
            weight_grads(g)
            copy = remote(parts.at[g], ry.at[i], rys.at[i], ryr.at[i], at(y + d, z))
            copy.start()
            rsends.append(copy)
    weight_grads(y_low)
    for copy in rsends:
        copy.wait_recv()

    def group_sum(k):
        total = parts[y_low, k].astype(f32)
        if groups == 4:
            total += ry[0, k].astype(f32) + ry[1, k].astype(f32)
            total += rh[k // half, k % half].astype(f32)
        return total

    zsends = []
    for d in [half] + [e for i in range(1, half) for e in (half - i, half + i)]:
        k = (z + d) % RING
        qbuf[k] = group_sum(k).astype(bf16)
        copy = remote(qbuf.at[k], rz.at[d - 1], rzs.at[d - 1], rzr.at[d - 1], at(y, z + d))
        copy.start()
        zsends.append(copy)
    result = group_sum(z)
    for d in range(1, RING):
        zsends[d - 1].wait_recv()
    for d in range(1, RING):
        result += rz[d - 1].astype(f32)
    if tiles == 2:
        rounded = result.astype(bf16)
        tbuf[...] = rounded
        tsend = remote(tbuf, rt, ts.at[0], tr.at[0], at(y + groups, z))
        tsend.start()
        tsend.wait_recv()
        result = rounded.astype(f32) + rt[...].astype(f32)
    up_out[:, 0:128] = result[0:40]
    up_out[:, 128:256] = result[40:80]
    up_out[:, 256:320] = result[160:200, 0:64]
    down_out[:, 0:128] = result[80:120]
    down_out[:, 128:256] = result[120:160]
    down_out[:, 256:320] = result[160:200, 64:128]

    for copy in pending + rsends + zsends:
        copy.wait_send()
    if tiles == 2:
        tsend.wait_send()

    @pl.when(s < last)
    def _():
        for m in range(micro):
            remote(obuf.at[m], xbuf.at[m], fs.at[m], fr.at[m], {"section": s + 1}).wait_send()

    @pl.when(s > 0)
    def _():
        for m in range(micro):
            remote(dsend.at[m], dybuf.at[m], bs.at[m], br.at[m], {"section": s - 1}).wait_send()


def local(features, labels, w_expand, w_reduce, head_weight):
    sections, shards, tiles = (lax.axis_size(a) for a in ("section", "fsdp", "tile"))
    groups = shards // RING
    micro, rows, width = features.shape
    hidden = 40 * shards
    loss_scale = 1.0 / math.sqrt(micro * rows * shards * tiles)
    vmem, dma = pltpu.VMEM, pltpu.SemaphoreType.DMA
    half = RING // 2

    def body(*refs):
        kernel(sections, groups, tiles, micro, loss_scale, *refs)

    up, down = pl.pallas_call(
        body,
        out_shape=[jax.ShapeDtypeStruct((40, width), f32)] * 2,
        in_specs=[pl.BlockSpec(memory_space=pltpu.VMEM)] * 5,
        out_specs=[pl.BlockSpec(memory_space=pltpu.VMEM)] * 2,
        scratch_shapes=[
            vmem((shards, PACK, LANES), bf16),
            vmem((hidden, 256), bf16),
            vmem((hidden, 256), bf16),
            vmem((hidden, LANES), bf16),
            vmem((width, hidden), bf16),
            vmem((width, hidden), bf16),
            vmem((width, LANES), bf16),
            vmem((micro, width, rows), bf16),
            vmem((micro, width, rows), bf16),
            vmem((micro, width, rows), bf16),
            vmem((micro, width, rows), f32),
            vmem((micro, 1, rows), f32),
            vmem((micro, hidden, rows), f32),
            vmem((micro, hidden, rows), bf16),
            vmem((micro, hidden, rows), bf16),
            vmem((micro, width, rows), bf16),
            vmem((micro, width, rows), bf16),
            vmem((groups, RING, PACK, LANES), bf16),
            vmem((2, RING, PACK, LANES), bf16),
            vmem((2, half, PACK, LANES), bf16),
            vmem((RING, PACK, LANES), bf16),
            vmem((RING - 1, PACK, LANES), bf16),
            vmem((PACK, LANES), bf16),
            vmem((PACK, LANES), bf16),
            dma((4,)),
            dma((groups * RING,)),
            dma((shards, 2)),
            dma((micro,)),
            dma((micro,)),
            dma((micro,)),
            dma((micro,)),
            dma((2,)),
            dma((2,)),
            dma((2,)),
            dma((2,)),
            dma((RING - 1,)),
            dma((RING - 1,)),
            dma((1,)),
            dma((1,)),
        ],
        compiler_params=pltpu.CompilerParams(
            collective_id=0, has_side_effects=True, vmem_limit_bytes=48 * 1024 * 1024
        ),
    )(features, labels, w_expand, w_reduce, head_weight)
    return up.T[None], down.T[None]


def solution(mesh):
    return jax.shard_map(
        local,
        mesh=mesh,
        in_specs=(
            P(None, ("fsdp", "tile"), None),
            P(None, ("fsdp", "tile")),
            P("section", None, "fsdp"),
            P("section", None, "fsdp"),
            P(),
        ),
        out_specs=(P("section", None, "fsdp"), P("section", None, "fsdp")),
        check_vma=False,
    )
```

time: 802 us -> 127 us (0.16)
  waiting for transfers between devices: 363 us -> 0 us
  blocking collectives: 142 us -> 0 us
  Pallas kernels: 0 us -> 122 us
  starting transfers between devices: 94.9 us -> 0 us
  matrix products: 90.7 us -> 0 us
  local copies, waits for them, and re-layouts: 45 us -> 4.17 us
  other arithmetic: 33.2 us -> 0 us
  loops' own time: 14.7 us -> 0 us
  between operations: 13.8 us -> 0.69 us
    unnamed x5 -> x0, waiting for transfers between devices: 293 us -> none
    all_gather x2 -> x0, blocking collectives: 142 us -> none  [the longest x1 77.4 us: local(): lax.all_gather(w_expand[0], 'fsdp', axis=1, tiled=True)]
    pallas_call x0 -> x1, Pallas kernels: none -> 122 us  [local(): pl.pallas_call(body, out_shape=[jax.ShapeDtypeStruct((40, width), f32)] *...]
    ppermute x22 -> x0, starting transfers between devices: 94.8 us -> none  [from_behind(): lax.ppermute(value, axis, [(source, source + steps) for source in range(l...]
    dot_general x88 -> x0, matrix products: 90.7 us -> none  [the longest x11 35.7 us: section_backward(): lax.dot_general(grad_out, hidden, (((0,), (0,)), ((), ())), preferred_ele...]
    psum x1 -> x0, waiting for transfers between devices: 63.6 us -> none  [local(): up_shard, down_shard = lax.psum((up_shard, down_shard), 'tile')]
    dynamic_slice x55 -> x0, local copies, waits for them, and re-layouts: 25.5 us -> none  [the longest x22 12.8 us: local(): lax.scan(forward_tick, (start_rows, start_inputs, start_pre, start_inputs...]
    another operation x2 -> x0, loops' own time: 14.7 us -> none  [the longest x1 7.76 us: local(): lax.scan(backward_tick, (start_rows, zero_grads, zero_grads), ticks_all)]
  transfers between devices with their start and end apart: 25 -> 0, of which waited for: 25 -> 0; matrix products, arithmetic and copies ran while one was open for 7% -> 0% of each run, Pallas kernels for 0% -> 0%
where the time goes in v1:
time: 127 us
  Pallas kernels  122 us (96%)
  local copies, waits for them, and re-layouts  4.17 us (3%)
    pallas_call x1, Pallas kernels, local(): pl.pallas_call(body, out_shape=[jax.ShapeDtypeStruct((40, width), f32)] *...  122 us
    unnamed x12, local copies, waits for them, and re-layouts  4.17 us

profile of v1, /device:TPU:1, one launch (start us, length us, event | category | flops | bytes accessed | tf_op | source)
XLA Modules:
  0.0 126.6 jit_solution(4763886049419374533)
XLA Ops:
  0.6 0.0 copy-start.1
  0.6 0.9 copy.8.refs_2_
  1.5 0.0 copy-done.1
  1.5 0.0 copy-start.2
  1.5 0.1 copy.9.refs_3_
  1.7 0.6 copy-done.2
  2.2 0.1 copy.10.refs_4_
  2.4 0.0 copy-start
  2.4 1.2 copy.7.refs_0_
  3.6 0.0 copy-done
  3.6 121.7 %shard_map.68 = (f32[40,320]{1,0:T(8,128)S(1)}, f32[40,320]{1,0:T(8,128)S(1)}) custom-call(bf16[4,128,320]{2,1,0:T(8,128)(2,1)S(1)} %copy.7.refs_0_, s32[4,128]{1,0:T(4,128)S(1)} %copy-done, bf16[1,320,40]{2,1,0:T(8,128)(2,1)S(1)} %copy.8.refs_2_, bf16[1,320,40]{2,1,0:T(8,128)(2,1)S(1)} %copy.9.refs_3_, bf16[320,5]{1,0:T(8,128)(2,1)S(1)} %copy.10.refs_4_), custom_call_target="tpu_custom_call" | custom-call | tf_op jit(solution)/shard_map/pallas_call | solution.py:403
  125.3 0.6 copy.13
  126.0 0.6 copy.14
Async XLA Ops:
  0.6 0.9 copy-start.1
  1.5 0.7 copy-start.2
  2.4 1.2 copy-start

commit v2 on v1

--- a/solution.py
+++ b/solution.py
@@ -12,6 +12,7 @@
 LANES = 128
 PACK = 208
 HALF = 112
+FIRST = 1
 GELU_C = math.sqrt(2.0 / math.pi)
 GELU_A = 0.044715
 bf16 = jnp.bfloat16
@@ -26,14 +27,16 @@
     return jnp.dot(lhs, rhs, preferred_element_type=f32)
 
 
-def tn(lhs, rhs):
-    return lax.dot_general(lhs, rhs, (((0,), (0,)), ((), ())), preferred_element_type=f32)
-
-
 def eye(size):
     row = lax.broadcasted_iota(jnp.int32, (size, size), 0)
     column = lax.broadcasted_iota(jnp.int32, (size, size), 1)
     return jnp.where(row == column, 1.0, 0.0).astype(bf16)
+
+
+def place(shift):
+    row = lax.broadcasted_iota(jnp.int32, (LANES, 64), 0)
+    column = lax.broadcasted_iota(jnp.int32, (LANES, 64), 1)
+    return jnp.where(row == column + shift, 1.0, 0.0).astype(bf16)
 
 
 def normalize(values):
@@ -69,12 +72,12 @@
 
 def kernel(
     sections, groups, tiles, micro, loss_scale,
-    feat, labels, wup, wdown, head,
+    feat_any, labels_any, wup_any, wdown_any, head_any,
     up_out, down_out,
-    gathered, up_t, down_t, mix_t, up_n, down_n, head_pad,
+    feat, labels, wup, wdown, head, gathered, up_t, down_t, mix_t, up_n, down_n, head_pad, head_n,
     xbuf, obuf, nbuf, ubuf, istd, pre, hid, gpre, dybuf, dsend,
-    parts, ry, rh, qbuf, rz, tbuf, rt,
-    gy_s, gz_s, g_r, fs, fr, bs, br, rys, ryr, rhs_, rhr, rzs, rzr, ts, tr,
+    parts, ry, rh, qbuf, rz, tbuf, rt, za, ysum, yall,
+    in_sem, g_s, g_r, fs, fr, bs, br, rys, ryr, rhs_, rhr, rzs, rzr, ts, tr, zs, zr, ys, yr,
 ):
     s = lax.axis_index("section")
     f = lax.axis_index("fsdp")
@@ -90,12 +93,18 @@
         z_new = (z_new + 2 * RING) % RING
         return {"fsdp": (y_new % groups) * RING + z_new, "tile": y_new // groups}
 
+    copies_in = [
+        pltpu.make_async_copy(source, target, in_sem.at[i])
+        for i, (source, target) in enumerate(
+            ((wup_any, wup), (wdown_any, wdown), (feat_any, feat), (labels_any, labels), (head_any, head))
+        )
+    ]
+    for copy in copies_in:
+        copy.start()
+
     barrier = pltpu.get_barrier_semaphore()
     partners = [at(y, z + d) for d in range(1, RING)]
-    if groups == 4:
-        partners += [at(y + d, z) for d in (1, -1, 2, -2)]
-    if tiles == 2:
-        partners.append(at(y + groups, z))
+    partners += [at(y + d, z) for d in range(1, height)]
     for device in partners:
         pl.semaphore_signal(barrier, inc=1, device_id=device, device_id_type=pl.DeviceIdType.MESH)
 
@@ -111,11 +120,12 @@
             barrier, inc=1, device_id={"section": s + 1}, device_id_type=pl.DeviceIdType.MESH
         )
 
-    up_w, down_w = wup[0], wdown[0]
-    stacked = jnp.concatenate([up_w[:256], down_w[:256], up_w[256:], down_w[256:]], axis=0)
-    own = nt(eye(40), stacked)
-    pieces = [own[:, LANES * i : LANES * (i + 1)] for i in range(5)]
-    pieces.append(jnp.zeros((8, LANES), f32))
+    for copy in copies_in[:2]:
+        copy.wait()
+    up_w, down_w = wup[...], wdown[...]
+    mixed = nt(up_w[:, 256:], place(0)) + nt(down_w[:, 256:], place(64))
+    pieces = [up_w[:, :128], up_w[:, 128:256], down_w[:, :128], down_w[:, 128:256]]
+    pieces = [piece.astype(f32) for piece in pieces] + [mixed, jnp.zeros((8, LANES), f32)]
     gathered[f] = jnp.concatenate(pieces, axis=0).astype(bf16)
 
     pl.semaphore_wait(
@@ -127,64 +137,98 @@
         return ((y_low + j) % groups) * RING + (z + dz + 2 * RING) % RING
 
     order = (0, 1, 3, 2) if groups == 4 else (0,)
-    pending = []
-    if groups == 4:
-        ysends = [
-            remote(gathered.at[f], gathered.at[f], gy_s.at[0], g_r.at[f, 0], at(y + 1, z)),
-            remote(gathered.at[f], gathered.at[f], gy_s.at[1], g_r.at[f, 0], at(y - 1, z)),
+    far = RING // 2
+    low_rows, high_rows = pl.ds(0, HALF), pl.ds(HALF, PACK - HALF)
+    is_a = s % 2 == FIRST
+
+    def arrived(index):
+        remote(
+            gathered.at[index], gathered.at[index], g_s.at[0], g_r.at[index, 0], at(y, z + 1)
+        ).wait_recv()
+
+    def halves_arrived(index):
+        for i, rows in enumerate((low_rows, high_rows)):
             remote(
-                gathered.at[f, pl.ds(0, HALF)], gathered.at[f, pl.ds(0, HALF)],
-                gy_s.at[2], g_r.at[f, 0], at(y + 2, z),
+                gathered.at[index, rows], gathered.at[index, rows],
+                g_s.at[0], g_r.at[index, i], at(y, z + 1),
+            ).wait_recv()
+
+    def y_sends(index, first):
+        if groups != 4:
+            return []
+        copies = [
+            remote(gathered.at[index], gathered.at[index], g_s.at[first], g_r.at[index, 0], at(y + 1, z)),
+            remote(gathered.at[index], gathered.at[index], g_s.at[first + 1], g_r.at[index, 0], at(y - 1, z)),
+            remote(
+                gathered.at[index, low_rows], gathered.at[index, low_rows],
+                g_s.at[first + 2], g_r.at[index, 0], at(y + 2, z),
             ),
             remote(
-                gathered.at[f, pl.ds(HALF, PACK - HALF)], gathered.at[f, pl.ds(HALF, PACK - HALF)],
-                gy_s.at[3], g_r.at[f, 1], at(y - 2, z),
+                gathered.at[index, high_rows], gathered.at[index, high_rows],
+                g_s.at[first + 3], g_r.at[index, 1], at(y - 2, z),
             ),
         ]
-        for copy in ysends:
+        for copy in copies:
             copy.start()
-        pending += ysends
-
-    def arrived(index):
-        remote(
-            gathered.at[index], gathered.at[index], gy_s.at[0], g_r.at[index, 0], at(y, z + 1)
-        ).wait_recv()
-
-    def ysend_arrived(index):
-        remote(
-            gathered.at[index, pl.ds(0, HALF)], gathered.at[index, pl.ds(0, HALF)],
-            gy_s.at[2], g_r.at[index, 0], at(y, z + 1),
-        ).wait_recv()
-        remote(
-            gathered.at[index, pl.ds(HALF, PACK - HALF)], gathered.at[index, pl.ds(HALF, PACK - HALF)],
-            gy_s.at[3], g_r.at[index, 1], at(y, z + 1),
-        ).wait_recv()
-
-    far = RING // 2
-    count = 0
-    for step in range(1, far + 1):
-        for place, j in enumerate(order):
-            if step == 1:
-                if j == 2:
-                    ysend_arrived(slot(j, 0))
-                elif j:
-                    arrived(slot(j, 0))
-            early = place < (len(order) + 1) // 2
-            for side in (1, -1):
-                index = slot(j, -side * (step - 1))
-                if step > 1:
+        return copies
+
+    @pl.when(is_a)
+    def _():
+        sent = y_sends(f, 0)
+
+        def z_send(index, d):
+            copy = remote(
+                gathered.at[index], gathered.at[index],
+                g_s.at[len(sent)], g_r.at[index, 0], at(y, z + d),
+            )
+            copy.start()
+            sent.append(copy)
+
+        for j in order:
+            if j:
+                (halves_arrived if j == 2 else arrived)(slot(j, 0))
+            for d in range(1, min(far, 2) + 1):
+                for side in (1, -1):
+                    if d == far and (j in order[: (len(order) + 1) // 2]) != (side == 1):
+                        continue
+                    z_send(slot(j, 0), side * d)
+        for step in range(2, far + 1):
+            for j in order:
+                early = j in order[: (len(order) + 1) // 2]
+                for side in (1, -1):
+                    index = slot(j, -side * (step - 1))
                     arrived(index)
-                if step == far and early != (side == 1):
-                    continue
-                copy = remote(
-                    gathered.at[index], gathered.at[index],
-                    gz_s.at[count], g_r.at[index, 0], at(y, z + side),
-                )
-                copy.start()
-                pending.append(copy)
-                count += 1
-    for j in order:
-        arrived(slot(j, far))
+                    if step < 3 or (step == far and early != (side == 1)):
+                        continue
+                    z_send(index, side)
+        for j in order:
+            arrived(slot(j, far))
+        for copy in sent:
+            copy.wait_send()
+
+    near_first = [d for i in range(1, far) for d in (i, -i)] + [far]
+
+    @pl.when(jnp.logical_not(is_a))
+    def _():
+        sent = []
+        for i, d in enumerate(near_first):
+            copy = remote(gathered.at[f], gathered.at[f], g_s.at[i], g_r.at[f, 0], at(y, z + d))
+            copy.start()
+            sent.append(copy)
+        sent += y_sends(f, len(sent))
+        for d in near_first:
+            arrived(slot(0, d))
+            sent += y_sends(slot(0, d), len(sent))
+        if groups == 4:
+            for d in [0] + near_first:
+                arrived(slot(1, d))
+                arrived(slot(3, d))
+                halves_arrived(slot(2, d))
+        for copy in sent:
+            copy.wait_send()
+
+    for copy in copies_in[2:]:
+        copy.wait()
 
     def unpack(pair, carry):
         first = gathered[2 * pair].astype(f32)
@@ -217,12 +261,13 @@
     @pl.when(s == 0)
     def _():
         for m in range(micro):
-            xbuf[m] = nt(eye(320), feat[m]).astype(bf16)
+            xbuf[m] = feat[m]
 
     @pl.when(s == last)
     def _():
         head_pad[...] = jnp.zeros_like(head_pad)
-        head_pad[:, 0:5] = head[...]
+        head_pad[0:5, :] = head[...]
+        head_n[...] = nt(eye(320), head_pad[...]).astype(bf16)
 
     def forward(m, carry):
         @pl.when(s > 0)
@@ -254,7 +299,7 @@
         @pl.when(s == last)
         def _():
             head_unit, head_istd = normalize(obuf[m])
-            logits = tn(head_pad[...], head_unit.astype(bf16))[0:8]
+            logits = nn(head_pad[0:16, :], head_unit.astype(bf16))[0:8]
             classes = lax.broadcasted_iota(jnp.int32, logits.shape, 0)
             exponent = jnp.where(classes < 5, jnp.exp(logits), 0.0)
             probs = exponent / jnp.sum(exponent, axis=0, keepdims=True)
@@ -263,7 +308,7 @@
             grad_logits = jnp.concatenate(
                 [grad_logits, jnp.zeros((LANES - 8, LANES), f32)], axis=0
             ).astype(bf16)
-            grad_norm = nn(head_pad[...], grad_logits)
+            grad_norm = nn(head_n[...], grad_logits)
             dybuf[m] = norm_back(head_unit, head_istd, grad_norm).astype(bf16)
 
         return carry
@@ -318,64 +363,121 @@
                  jnp.zeros((8, LANES), f32)], axis=0,
             ).astype(bf16)
 
-    half = RING // 2
-    rsends = []
-    if groups == 4:
-        g = (y_low + 2) % groups
-        weight_grads(g)
-        rsends += [
-            remote(parts.at[g, pl.ds(0, half)], rh.at[0], rhs_.at[0], rhr.at[0], at(y - 2, z)),
-            remote(parts.at[g, pl.ds(half, half)], rh.at[1], rhs_.at[1], rhr.at[1], at(y + 2, z)),
-        ]
-        rsends[0].start()
-        rsends[1].start()
-        for i, d in enumerate((1, -1)):
-            g = (y_low + d + groups) % groups
+    def write(result):
+        up_out[:, 0:128] = result[0:40]
+        up_out[:, 128:256] = result[40:80]
+        up_out[:, 256:320] = result[160:200, 0:64]
+        down_out[:, 0:128] = result[80:120]
+        down_out[:, 128:256] = result[120:160]
+        down_out[:, 256:320] = result[160:200, 64:128]
+
+    @pl.when(is_a)
+    def _():
+        for g in range(groups):
             weight_grads(g)
-            copy = remote(parts.at[g], ry.at[i], rys.at[i], ryr.at[i], at(y + d, z))
+        sent = []
+        for step in range(1, far + 1):
+            for where in range(groups):
+                g = (y_low + where) % groups
+                early = where < (groups + 1) // 2
+                for i, side in enumerate((1, -1)):
+                    if step == 1 and early != (side == 1):
+                        continue
+                    k = (z + side * (far + 1 - step) + RING) % RING
+                    source = parts.at[g, k]
+                    if step > 2 or (step == 2 and early == (side == 1)):
+                        source = za.at[i, step - 2, where]
+                        remote(source, source, zs.at[0], zr.at[i, step - 2, where], at(y, z + 1)).wait_recv()
+                        source[...] = (source[...].astype(f32) + parts[g, k].astype(f32)).astype(bf16)
+                    copy = remote(
+                        source, za.at[i, step - 1, where],
+                        zs.at[len(sent)], zr.at[i, step - 1, where], at(y, z + side),
+                    )
+                    copy.start()
+                    sent.append(copy)
+        for where in ((0, 2, 1, 3) if groups == 4 else range(groups)):
+            g = (y_low + where) % groups
+            early = where < (groups + 1) // 2
+            total = parts[g, z].astype(f32)
+            for i, side in enumerate((1, -1)):
+                if far == 1 and early != (side == 1):
+                    continue
+                source = za.at[i, far - 1, where]
+                remote(source, source, zs.at[0], zr.at[i, far - 1, where], at(y, z + 1)).wait_recv()
+                total += source[...].astype(f32)
+            ysum[where] = total.astype(bf16)
+            for e in range(1, height):
+                if e % groups == where:
+                    copy = remote(ysum.at[where], yall.at[y], ys.at[e], yr.at[y], at(y + e, z))
+                    copy.start()
+                    sent.append(copy)
+        yall[y] = ysum[0]
+        for e in range(1, height):
+            source = yall.at[(y + e) % height]
+            remote(source, source, ys.at[0], yr.at[(y + e) % height], at(y, z + 1)).wait_recv()
+        total = yall[0].astype(f32)
+        for e in range(1, height):
+            total += yall[e].astype(f32)
+        write(total)
+        for copy in sent:
+            copy.wait_send()
+
+    @pl.when(jnp.logical_not(is_a))
+    def _():
+        sent = []
+        far_first = [far] + [d for i in range(1, far) for d in (far - i, far + i)]
+        if groups == 4:
+            g = (y_low + 2) % groups
+            weight_grads(g)
+            for d in far_first + [0]:
+                k = (z + d) % RING
+                copy = remote(
+                    parts.at[g, k], rh.at[k], rhs_.at[d], rhr.at[k],
+                    at(y + jnp.where(k < far, -2, 2), z),
+                )
+                copy.start()
+                sent.append(copy)
+            for g in ((y_low + 1) % groups, (y_low + 3) % groups):
+                weight_grads(g)
+            for d in far_first + [0]:
+                k = (z + d) % RING
+                for i, side in enumerate((1, -1)):
+                    g = (y_low + side + groups) % groups
+                    copy = remote(parts.at[g, k], ry.at[i, k], rys.at[i, d], ryr.at[i, k], at(y + side, z))
+                    copy.start()
+                    sent.append(copy)
+        weight_grads(y_low)
+
+        def group_sum(k):
+            total = parts[y_low, k].astype(f32)
+            if groups == 4:
+                remote(rh.at[k], rh.at[k], rhs_.at[0], rhr.at[k], at(y, z + 1)).wait_recv()
+                for i in range(2):
+                    remote(ry.at[i, k], ry.at[i, k], rys.at[i, 0], ryr.at[i, k], at(y, z + 1)).wait_recv()
+                total += ry[0, k].astype(f32) + ry[1, k].astype(f32) + rh[k].astype(f32)
+            return total
+
+        for d in far_first:
+            k = (z + d) % RING
+            qbuf[k] = group_sum(k).astype(bf16)
+            copy = remote(qbuf.at[k], rz.at[d - 1], rzs.at[d - 1], rzr.at[d - 1], at(y, z + d))
             copy.start()
-            rsends.append(copy)
-    weight_grads(y_low)
-    for copy in rsends:
-        copy.wait_recv()
-
-    def group_sum(k):
-        total = parts[y_low, k].astype(f32)
-        if groups == 4:
-            total += ry[0, k].astype(f32) + ry[1, k].astype(f32)
-            total += rh[k // half, k % half].astype(f32)
-        return total
-
-    zsends = []
-    for d in [half] + [e for i in range(1, half) for e in (half - i, half + i)]:
-        k = (z + d) % RING
-        qbuf[k] = group_sum(k).astype(bf16)
-        copy = remote(qbuf.at[k], rz.at[d - 1], rzs.at[d - 1], rzr.at[d - 1], at(y, z + d))
-        copy.start()
-        zsends.append(copy)
-    result = group_sum(z)
-    for d in range(1, RING):
-        zsends[d - 1].wait_recv()
-    for d in range(1, RING):
-        result += rz[d - 1].astype(f32)
-    if tiles == 2:
-        rounded = result.astype(bf16)
-        tbuf[...] = rounded
-        tsend = remote(tbuf, rt, ts.at[0], tr.at[0], at(y + groups, z))
-        tsend.start()
-        tsend.wait_recv()
-        result = rounded.astype(f32) + rt[...].astype(f32)
-    up_out[:, 0:128] = result[0:40]
-    up_out[:, 128:256] = result[40:80]
-    up_out[:, 256:320] = result[160:200, 0:64]
-    down_out[:, 0:128] = result[80:120]
-    down_out[:, 128:256] = result[120:160]
-    down_out[:, 256:320] = result[160:200, 64:128]
-
-    for copy in pending + rsends + zsends:
-        copy.wait_send()
-    if tiles == 2:
-        tsend.wait_send()
+            sent.append(copy)
+        result = group_sum(z)
+        for d in range(1, RING):
+            remote(rz.at[d - 1], rz.at[d - 1], rzs.at[0], rzr.at[d - 1], at(y, z + 1)).wait_recv()
+            result += rz[d - 1].astype(f32)
+        if tiles == 2:
+            rounded = result.astype(bf16)
+            tbuf[...] = rounded
+            copy = remote(tbuf, rt, ts.at[0], tr.at[0], at(y + groups, z))
+            copy.start()
+            sent.append(copy)
+            copy.wait_recv()
+            result = rounded.astype(f32) + rt[...].astype(f32)
+        write(result)
+        for copy in sent:
+            copy.wait_send()
 
     @pl.when(s < last)
     def _():
@@ -403,15 +505,21 @@
     up, down = pl.pallas_call(
         body,
         out_shape=[jax.ShapeDtypeStruct((40, width), f32)] * 2,
-        in_specs=[pl.BlockSpec(memory_space=pltpu.VMEM)] * 5,
+        in_specs=[pl.BlockSpec(memory_space=pl.ANY)] * 5,
         out_specs=[pl.BlockSpec(memory_space=pltpu.VMEM)] * 2,
         scratch_shapes=[
+            vmem((micro, width, rows), bf16),
+            vmem((micro, rows), jnp.int32),
+            vmem((40, width), bf16),
+            vmem((40, width), bf16),
+            vmem((5, width), bf16),
             vmem((shards, PACK, LANES), bf16),
             vmem((hidden, 256), bf16),
             vmem((hidden, 256), bf16),
             vmem((hidden, LANES), bf16),
             vmem((width, hidden), bf16),
             vmem((width, hidden), bf16),
+            vmem((LANES, width), bf16),
             vmem((width, LANES), bf16),
             vmem((micro, width, rows), bf16),
             vmem((micro, width, rows), bf16),
@@ -425,31 +533,38 @@
             vmem((micro, width, rows), bf16),
             vmem((groups, RING, PACK, LANES), bf16),
             vmem((2, RING, PACK, LANES), bf16),
-            vmem((2, half, PACK, LANES), bf16),
+            vmem((RING, PACK, LANES), bf16),
             vmem((RING, PACK, LANES), bf16),
             vmem((RING - 1, PACK, LANES), bf16),
             vmem((PACK, LANES), bf16),
             vmem((PACK, LANES), bf16),
-            dma((4,)),
-            dma((groups * RING,)),
+            vmem((2, half, groups, PACK, LANES), bf16),
+            vmem((groups, PACK, LANES), bf16),
+            vmem((groups * tiles, PACK, LANES), bf16),
+            dma((5,)),
+            dma((7 * RING,)),
             dma((shards, 2)),
             dma((micro,)),
             dma((micro,)),
             dma((micro,)),
             dma((micro,)),
-            dma((2,)),
-            dma((2,)),
-            dma((2,)),
-            dma((2,)),
+            dma((2, RING)),
+            dma((2, RING)),
+            dma((RING,)),
+            dma((RING,)),
             dma((RING - 1,)),
             dma((RING - 1,)),
             dma((1,)),
             dma((1,)),
+            dma((groups * RING,)),
+            dma((2, half, groups)),
+            dma((groups * tiles,)),
+            dma((groups * tiles,)),
         ],
         compiler_params=pltpu.CompilerParams(
-            collective_id=0, has_side_effects=True, vmem_limit_bytes=48 * 1024 * 1024
+            collective_id=0, has_side_effects=True, vmem_limit_bytes=60 * 1024 * 1024
         ),
-    )(features, labels, w_expand, w_reduce, head_weight)
+    )(features.transpose(0, 2, 1), labels, w_expand[0].T, w_reduce[0].T, head_weight.T)
     return up.T[None], down.T[None]
 
 

time: 127 us -> 110 us (0.87)
  Pallas kernels: 122 us -> 107 us
  local copies, waits for them, and re-layouts: 4.17 us -> 2.1 us
    pallas_call x1, Pallas kernels: 122 us -> 107 us  [local(): pl.pallas_call(body, out_shape=[jax.ShapeDtypeStruct((40, width), f32)] *...]
    unnamed x12 -> x4, local copies, waits for them, and re-layouts: 4.17 us -> 2.1 us
where the time goes in v2:
time: 110 us; the launch traced here: 109 us
  Pallas kernels  107 us (97%)
  local copies, waits for them, and re-layouts  2.1 us (2%)
    pallas_call x1, Pallas kernels, local(): pl.pallas_call(body, out_shape=[jax.ShapeDtypeStruct((40, width), f32)] *...  107 us

profile of v2, /device:TPU:1, one launch (start us, length us, event | category | flops | bytes accessed | tf_op | source)
XLA Modules:
  0.0 109.5 jit_solution(7095848597249224511)
XLA Ops:
  0.6 106.7 %shard_map.68 = (f32[40,320]{1,0:T(8,128)}, f32[40,320]{1,0:T(8,128)}) custom-call(bf16[4,320,128]{2,1,0:T(8,128)(2,1)} %bitcast.14, s32[4,128]{1,0:T(4,128)} %refs_1_.1, bf16[40,320]{1,0:T(8,128)(2,1)} %bitcast.17, bf16[40,320]{1,0:T(8,128)(2,1)} %bitcast.18, bf16[5,320]{1,0:T(8,128)(2,1)} %bitcast.19), custom_call_target="tpu_custom_call" | custom-call | tf_op jit(solution)/shard_map/pallas_call | solution.py:505
  107.4 0.0 copy-start
  107.4 1.5 %copy.9 = f32[1,320,40]{1,2,0:T(8,128)} copy(f32[1,320,40]{1,2,0:T(8,128)} %bitcast.16) | data formatting | bytes 102400
  108.8 0.0 copy-done
  108.8 0.6 copy.10
Async XLA Ops:
  107.4 1.5 %copy-start = (f32[40,320]{1,0:T(8,128)S(1)}, f32[40,320]{1,0:T(8,128)}, u32[]{:S(2)}) copy-start(f32[40,320]{1,0:T(8,128)} %get-tuple-element.5) | copy-start | bytes 153604

commit v3 on v2

--- a/solution.py
+++ b/solution.py
@@ -13,6 +13,7 @@
 PACK = 208
 HALF = 112
 FIRST = 1
+FIRST_SUM = 1
 GELU_C = math.sqrt(2.0 / math.pi)
 GELU_A = 0.044715
 bf16 = jnp.bfloat16
@@ -73,7 +74,7 @@
 def kernel(
     sections, groups, tiles, micro, loss_scale,
     feat_any, labels_any, wup_any, wdown_any, head_any,
-    up_out, down_out,
+    both_out,
     feat, labels, wup, wdown, head, gathered, up_t, down_t, mix_t, up_n, down_n, head_pad, head_n,
     xbuf, obuf, nbuf, ubuf, istd, pre, hid, gpre, dybuf, dsend,
     parts, ry, rh, qbuf, rz, tbuf, rt, za, ysum, yall,
@@ -87,6 +88,8 @@
     y = t * groups + y_low
     last = sections - 1
     block = 40 * RING
+    hidden = block * groups
+    fine = math.gcd(hidden, 128)
 
     def at(y_new, z_new):
         y_new = (y_new + 2 * height) % height
@@ -140,6 +143,7 @@
     far = RING // 2
     low_rows, high_rows = pl.ds(0, HALF), pl.ds(HALF, PACK - HALF)
     is_a = s % 2 == FIRST
+    sum_a = s % 2 == FIRST_SUM
 
     def arrived(index):
         remote(
@@ -184,23 +188,37 @@
             copy.start()
             sent.append(copy)
 
-        for j in order:
-            if j:
-                (halves_arrived if j == 2 else arrived)(slot(j, 0))
-            for d in range(1, min(far, 2) + 1):
-                for side in (1, -1):
-                    if d == far and (j in order[: (len(order) + 1) // 2]) != (side == 1):
-                        continue
-                    z_send(slot(j, 0), side * d)
-        for step in range(2, far + 1):
-            for j in order:
-                early = j in order[: (len(order) + 1) // 2]
-                for side in (1, -1):
-                    index = slot(j, -side * (step - 1))
-                    arrived(index)
-                    if step < 3 or (step == far and early != (side == 1)):
-                        continue
+        def is_early(j):
+            return j in order[: (len(order) + 1) // 2]
+
+        def spread(j):
+            for side in (1, -1):
+                if far > 1 or is_early(j) == (side == 1):
+                    z_send(slot(j, 0), side)
+
+        def forward_from(j, distance):
+            for side in (1, -1):
+                index = slot(j, -side * distance)
+                arrived(index)
+                if distance + 1 < far or is_early(j) == (side == 1):
                     z_send(index, side)
+
+        spread(0)
+        for j in order[1:3]:
+            arrived(slot(j, 0))
+            spread(j)
+        if far > 1:
+            forward_from(0, 1)
+        if len(order) > 3:
+            halves_arrived(slot(2, 0))
+            spread(2)
+        if far > 1:
+            for j in order[1:]:
+                forward_from(j, 1)
+        if far > 2:
+            for distance in (2, 3):
+                for j in (0,) + order[1:]:
+                    forward_from(j, distance)
         for j in order:
             arrived(slot(j, far))
         for copy in sent:
@@ -211,14 +229,28 @@
     @pl.when(jnp.logical_not(is_a))
     def _():
         sent = []
-        for i, d in enumerate(near_first):
-            copy = remote(gathered.at[f], gathered.at[f], g_s.at[i], g_r.at[f, 0], at(y, z + d))
+
+        def z_send(index, d, rows=None, half=0):
+            ref = gathered.at[index] if rows is None else gathered.at[index, rows]
+            copy = remote(ref, ref, g_s.at[len(sent)], g_r.at[index, half], at(y, z + d))
             copy.start()
             sent.append(copy)
+
+        for d in near_first:
+            if abs(d) <= 2:
+                z_send(f, d)
         sent += y_sends(f, len(sent))
         for d in near_first:
-            arrived(slot(0, d))
-            sent += y_sends(slot(0, d), len(sent))
+            index = slot(0, d)
+            if abs(d) == 4:
+                halves_arrived(index)
+            else:
+                arrived(index)
+            if abs(d) == 2 and far == 4:
+                side = -d // 2
+                z_send(index, side)
+                z_send(index, 2 * side, low_rows if side == 1 else high_rows, 0 if side == 1 else 1)
+            sent += y_sends(index, len(sent))
         if groups == 4:
             for d in [0] + near_first:
                 arrived(slot(1, d))
@@ -282,13 +314,12 @@
         nbuf[m] = normed
         low, high = normed[:256], low_pad(normed[256:])
         total = x.astype(f32)
-        for g in range(groups):
-            rows = slice(block * g, block * (g + 1))
+        for first in range(0, hidden, fine):
+            rows = slice(first, first + fine)
             before = nn(up_t[rows, :], low) + nn(mix_t[rows, :], high)
             pre[m, rows, :] = before
             bent = jnp.tanh(GELU_C * (before + GELU_A * (before * before * before)))
-            hidden = (before * (0.5 * (1.0 + bent))).astype(bf16)
-            hid[m, rows, :] = hidden
+            hid[m, rows, :] = (before * (0.5 * (1.0 + bent))).astype(bf16)
         out = (total + nn(down_n[...], hid[m])).astype(bf16)
         obuf[m] = out
 
@@ -322,14 +353,15 @@
 
         dy = dybuf[m]
         low, high = dy[:256], high_pad(dy[256:])
-        for g in range(groups):
-            rows = slice(block * g, block * (g + 1))
+        for first in range(0, hidden, fine // 2):
+            rows = slice(first, first + fine // 2)
             grad_hidden = nn(down_t[rows, :], low) + nn(mix_t[rows, :], high)
             before = pre[m, rows, :]
             square = before * before
-            bent = jnp.tanh(GELU_C * (before + GELU_A * (square * before)))
-            slope = 0.5 * (1.0 + bent) + (0.5 * before) * (1.0 - bent * bent) * (
-                GELU_C * (1.0 + (3.0 * GELU_A) * square)
+            bent = jnp.tanh(before * (GELU_C + (GELU_C * GELU_A) * square))
+            share = 0.5 + 0.5 * bent
+            slope = share + (share * (1.0 - bent)) * (
+                before * (GELU_C + (3.0 * GELU_C * GELU_A) * square)
             )
             gpre[m, rows, :] = (grad_hidden * slope).astype(bf16)
 
@@ -352,10 +384,10 @@
     def weight_grads(g):
         rows = pl.ds(pl.multiple_of(g * block, 16), block)
         grad_pre = jnp.concatenate([gpre[m, rows, :] for m in range(micro)], axis=1)
-        hidden = jnp.concatenate([hid[m, rows, :] for m in range(micro)], axis=1)
+        active = jnp.concatenate([hid[m, rows, :] for m in range(micro)], axis=1)
         up = nt(grad_pre, normed_low)
-        down = nt(hidden, grads_low)
-        mix = nt(grad_pre, normed_high) + nt(hidden, grads_high)
+        down = nt(active, grads_low)
+        mix = nt(grad_pre, normed_high) + nt(active, grads_high)
         for k in range(RING):
             r = slice(40 * k, 40 * k + 40)
             parts[g, k] = jnp.concatenate(
@@ -364,47 +396,68 @@
             ).astype(bf16)
 
     def write(result):
-        up_out[:, 0:128] = result[0:40]
-        up_out[:, 128:256] = result[40:80]
-        up_out[:, 256:320] = result[160:200, 0:64]
-        down_out[:, 0:128] = result[80:120]
-        down_out[:, 128:256] = result[120:160]
-        down_out[:, 256:320] = result[160:200, 64:128]
-
-    @pl.when(is_a)
-    def _():
-        for g in range(groups):
-            weight_grads(g)
+        both_out[0:40, 0:128] = result[0:40]
+        both_out[0:40, 128:256] = result[40:80]
+        both_out[0:40, 256:320] = result[160:200, 0:64]
+        both_out[40:80, 0:128] = result[80:120]
+        both_out[40:80, 128:256] = result[120:160]
+        both_out[40:80, 256:320] = result[160:200, 64:128]
+
+    @pl.when(sum_a)
+    def _():
         sent = []
-        for step in range(1, far + 1):
+        sides = tuple(enumerate((1, -1)))
+
+        def is_early(where):
+            return where < (groups + 1) // 2
+
+        def pass_on(i, side, where, distance, level, hops, add=None):
+            g = (y_low + where) % groups
+            k = (z + side * distance + RING) % RING
+            source = parts.at[g, k]
+            if add is not None:
+                source = za.at[i, add, where]
+                remote(source, source, zs.at[0], zr.at[i, add, where], at(y, z + 1)).wait_recv()
+                source[...] = (source[...].astype(f32) + parts[g, k].astype(f32)).astype(bf16)
+            copy = remote(
+                source, za.at[i, level, where],
+                zs.at[len(sent)], zr.at[i, level, where], at(y, z + side * hops),
+            )
+            copy.start()
+            sent.append(copy)
+
+        for where in range(groups):
+            weight_grads((y_low + where) % groups)
+            if far == 4:
+                for i, side in sides:
+                    if is_early(where) == (side == 1):
+                        pass_on(i, side, where, 4, 0, 1)
+                    else:
+                        pass_on(i, side, where, 3, 1, 1)
+        for where in range(groups):
+            for i, side in sides:
+                if far == 4 or is_early(where) == (side == 1):
+                    pass_on(i, side, where, 1, far - 1, 1)
+        if far == 4:
             for where in range(groups):
-                g = (y_low + where) % groups
-                early = where < (groups + 1) // 2
-                for i, side in enumerate((1, -1)):
-                    if step == 1 and early != (side == 1):
-                        continue
-                    k = (z + side * (far + 1 - step) + RING) % RING
-                    source = parts.at[g, k]
-                    if step > 2 or (step == 2 and early == (side == 1)):
-                        source = za.at[i, step - 2, where]
-                        remote(source, source, zs.at[0], zr.at[i, step - 2, where], at(y, z + 1)).wait_recv()
-                        source[...] = (source[...].astype(f32) + parts[g, k].astype(f32)).astype(bf16)
-                    copy = remote(
-                        source, za.at[i, step - 1, where],
-                        zs.at[len(sent)], zr.at[i, step - 1, where], at(y, z + side),
-                    )
-                    copy.start()
-                    sent.append(copy)
+                for i, side in sides:
+                    if is_early(where) == (side == 1):
+                        pass_on(i, side, where, 3, 1, 1, add=0)
+            for late in (True, False):
+                for where in range(groups):
+                    for i, side in sides:
+                        if (is_early(where) != (side == 1)) == late:
+                            pass_on(i, side, where, 2, 2, 2, add=1)
         for where in ((0, 2, 1, 3) if groups == 4 else range(groups)):
             g = (y_low + where) % groups
-            early = where < (groups + 1) // 2
             total = parts[g, z].astype(f32)
-            for i, side in enumerate((1, -1)):
-                if far == 1 and early != (side == 1):
-                    continue
-                source = za.at[i, far - 1, where]
-                remote(source, source, zs.at[0], zr.at[i, far - 1, where], at(y, z + 1)).wait_recv()
-                total += source[...].astype(f32)
+            for i, side in sides:
+                for level in ((2, 3) if far == 4 else (0,)):
+                    if far == 1 and is_early(where) != (side == 1):
+                        continue
+                    source = za.at[i, level, where]
+                    remote(source, source, zs.at[0], zr.at[i, level, where], at(y, z + 1)).wait_recv()
+                    total += source[...].astype(f32)
             ysum[where] = total.astype(bf16)
             for e in range(1, height):
                 if e % groups == where:
@@ -422,7 +475,7 @@
         for copy in sent:
             copy.wait_send()
 
-    @pl.when(jnp.logical_not(is_a))
+    @pl.when(jnp.logical_not(sum_a))
     def _():
         sent = []
         far_first = [far] + [d for i in range(1, far) for d in (far - i, far + i)]
@@ -502,11 +555,11 @@
     def body(*refs):
         kernel(sections, groups, tiles, micro, loss_scale, *refs)
 
-    up, down = pl.pallas_call(
+    both = pl.pallas_call(
         body,
-        out_shape=[jax.ShapeDtypeStruct((40, width), f32)] * 2,
+        out_shape=jax.ShapeDtypeStruct((80, width), f32),
         in_specs=[pl.BlockSpec(memory_space=pl.ANY)] * 5,
-        out_specs=[pl.BlockSpec(memory_space=pltpu.VMEM)] * 2,
+        out_specs=pl.BlockSpec(memory_space=pltpu.VMEM),
         scratch_shapes=[
             vmem((micro, width, rows), bf16),
             vmem((micro, rows), jnp.int32),
@@ -565,7 +618,7 @@
             collective_id=0, has_side_effects=True, vmem_limit_bytes=60 * 1024 * 1024
         ),
     )(features.transpose(0, 2, 1), labels, w_expand[0].T, w_reduce[0].T, head_weight.T)
-    return up.T[None], down.T[None]
+    return both[:40].T[None], both[40:].T[None]
 
 
 def solution(mesh):

time: 110 us -> 104 us (0.945)
  the two profiles are of different devices: /device:TPU:1 before, /device:TPU:8 now
where the time goes in v3:
time: 104 us
  Pallas kernels  102 us (98%)
  local copies, waits for them, and re-layouts  1.51 us (1%)
    pallas_call x1, Pallas kernels, local(): pl.pallas_call(body, out_shape=jax.ShapeDtypeStruct((80, width), f32), in...  102 us

profile of v3, /device:TPU:8, one launch (start us, length us, event | category | flops | bytes accessed | tf_op | source)
XLA Modules:
  0.0 103.9 jit_solution(14952897698879645614)
XLA Ops:
  0.6 101.7 %shard_map.68 = f32[80,320]{1,0:T(8,128)} custom-call(bf16[4,320,128]{2,1,0:T(8,128)(2,1)} %bitcast.16, s32[4,128]{1,0:T(4,128)} %refs_1_.1, bf16[40,320]{1,0:T(8,128)(2,1)} %bitcast.17, bf16[40,320]{1,0:T(8,128)(2,1)} %bitcast.18, bf16[5,320]{1,0:T(8,128)(2,1)} %bitcast.19), custom_call_target="tpu_custom_call" | custom-call | tf_op jit(solution)/shard_map/pallas_call | solution.py:558
  102.4 1.5 %slice_bitcast_fusion = (f32[1,320,40]{1,2,0:T(8,128)}, f32[1,320,40]{1,2,0:T(8,128)}) fusion(f32[80,320]{1,0:T(8,128)} %shard_map.68), kind=kLoop, calls=%fused_computation | loop fusion | bytes 204800 | tf_op jit(solution)/shard_map/broadcast_in_dim | solution.py:621

commit v4 on v3

--- a/solution.py
+++ b/solution.py
@@ -106,8 +106,10 @@
         copy.start()
 
     barrier = pltpu.get_barrier_semaphore()
-    partners = [at(y, z + d) for d in range(1, RING)]
-    partners += [at(y + d, z) for d in range(1, height)]
+    def near(size):
+        return (1, -1, 2, -2) if size > 4 else range(1, size)
+
+    partners = [at(y, z + d) for d in near(RING)] + [at(y + d, z) for d in near(height)]
     for device in partners:
         pl.semaphore_signal(barrier, inc=1, device_id=device, device_id_type=pl.DeviceIdType.MESH)
 
@@ -176,6 +178,32 @@
             copy.start()
         return copies
 
+    def unpack(pair, carry):
+        first = gathered[2 * pair].astype(f32)
+        second = gathered[2 * pair + 1].astype(f32)
+        rows = pl.ds(pl.multiple_of(pair * 80, 16), 80)
+
+        def both(i):
+            return jnp.concatenate(
+                [first[40 * i : 40 * i + 40], second[40 * i : 40 * i + 40]], axis=0
+            ).astype(bf16)
+
+        up_t[rows, 0:128] = both(0)
+        up_t[rows, 128:256] = both(1)
+        down_t[rows, 0:128] = both(2)
+        down_t[rows, 128:256] = both(3)
+        mix_t[rows, :] = both(4)
+        return carry
+
+    pairs = RING // 2
+    soon, late = ((0, 1, 3), 2) if far == 4 else ((), 0)
+
+    def unpack_column(r):
+        def one(j, carry):
+            return unpack((y_low + j) % groups * pairs + (z // 2 + r) % pairs, carry)
+
+        lax.fori_loop(0, groups, one, 0)
+
     @pl.when(is_a)
     def _():
         sent = y_sends(f, 0)
@@ -219,8 +247,11 @@
             for distance in (2, 3):
                 for j in (0,) + order[1:]:
                     forward_from(j, distance)
+        for r in soon:
+            unpack_column(r)
         for j in order:
             arrived(slot(j, far))
+        unpack_column(late)
         for copy in sent:
             copy.wait_send()
 
@@ -236,50 +267,36 @@
             copy.start()
             sent.append(copy)
 
-        for d in near_first:
-            if abs(d) <= 2:
-                z_send(f, d)
+        for d in (2, -2, 1, -1) if far == 4 else near_first:
+            z_send(f, d)
         sent += y_sends(f, len(sent))
+        if far == 4:
+            for side in (1, -1):
+                index = slot(0, -2 * side)
+                arrived(index)
+                z_send(index, side)
+                z_send(index, 2 * side, low_rows if side == 1 else high_rows, 0 if side == 1 else 1)
         for d in near_first:
             index = slot(0, d)
             if abs(d) == 4:
                 halves_arrived(index)
-            else:
+            elif abs(d) != 2:
                 arrived(index)
-            if abs(d) == 2 and far == 4:
-                side = -d // 2
-                z_send(index, side)
-                z_send(index, 2 * side, low_rows if side == 1 else high_rows, 0 if side == 1 else 1)
             sent += y_sends(index, len(sent))
-        if groups == 4:
-            for d in [0] + near_first:
-                arrived(slot(1, d))
-                arrived(slot(3, d))
-                halves_arrived(slot(2, d))
+        for r in soon + (late,):
+            if groups == 4:
+                first = (z // 2 + r) % pairs * 2
+                for j in (1, 3, 2):
+                    for index in (first, first + 1):
+                        index += (y_low + j) % groups * RING
+                        (halves_arrived if j == 2 else arrived)(index)
+            unpack_column(r)
         for copy in sent:
             copy.wait_send()
 
     for copy in copies_in[2:]:
         copy.wait()
 
-    def unpack(pair, carry):
-        first = gathered[2 * pair].astype(f32)
-        second = gathered[2 * pair + 1].astype(f32)
-        rows = pl.ds(pl.multiple_of(pair * 80, 16), 80)
-
-        def both(i):
-            return jnp.concatenate(
-                [first[40 * i : 40 * i + 40], second[40 * i : 40 * i + 40]], axis=0
-            ).astype(bf16)
-
-        up_t[rows, 0:128] = both(0)
-        up_t[rows, 128:256] = both(1)
-        down_t[rows, 0:128] = both(2)
-        down_t[rows, 128:256] = both(3)
-        mix_t[rows, :] = both(4)
-        return carry
-
-    lax.fori_loop(0, groups * RING // 2, unpack, 0)
     wide = eye(256)
     down_n[0:256, :] = nt(wide, down_t[...]).astype(bf16)
     turned = nt(eye(128), mix_t[...]).astype(bf16)
@@ -327,24 +344,25 @@
         def _():
             remote(obuf.at[m], xbuf.at[m], fs.at[m], fr.at[m], {"section": s + 1}).start()
 
-        @pl.when(s == last)
-        def _():
+        return carry
+
+    lax.fori_loop(0, micro, forward, 0)
+
+    @pl.when(s == last)
+    def _():
+        for m in range(micro):
             head_unit, head_istd = normalize(obuf[m])
             logits = nn(head_pad[0:16, :], head_unit.astype(bf16))[0:8]
             classes = lax.broadcasted_iota(jnp.int32, logits.shape, 0)
             exponent = jnp.where(classes < 5, jnp.exp(logits), 0.0)
             probs = exponent / jnp.sum(exponent, axis=0, keepdims=True)
-            onehot = jnp.where(classes == labels[pl.ds(m, 1), :], 1.0, 0.0)
+            onehot = jnp.where(classes == labels[m : m + 1, :], 1.0, 0.0)
             grad_logits = (probs - onehot) * loss_scale
             grad_logits = jnp.concatenate(
                 [grad_logits, jnp.zeros((LANES - 8, LANES), f32)], axis=0
             ).astype(bf16)
             grad_norm = nn(head_n[...], grad_logits)
             dybuf[m] = norm_back(head_unit, head_istd, grad_norm).astype(bf16)
-
-        return carry
-
-    lax.fori_loop(0, micro, forward, 0)
 
     def backward(m, carry):
         @pl.when(s < last)
@@ -480,34 +498,50 @@
         sent = []
         far_first = [far] + [d for i in range(1, far) for d in (far - i, far + i)]
         if groups == 4:
-            g = (y_low + 2) % groups
-            weight_grads(g)
+            two = (y_low + 2) % groups
+            weight_grads(two)
             for d in far_first + [0]:
                 k = (z + d) % RING
                 copy = remote(
-                    parts.at[g, k], rh.at[k], rhs_.at[d], rhr.at[k],
-                    at(y + jnp.where(k < far, -2, 2), z),
+                    parts.at[two, k], rh.at[k], rhs_.at[d], rhr.at[k],
+                    at(y + jnp.where(k < far, -1, 1), z),
                 )
                 copy.start()
                 sent.append(copy)
             for g in ((y_low + 1) % groups, (y_low + 3) % groups):
                 weight_grads(g)
-            for d in far_first + [0]:
+
+            def to_owner(d, relayed):
                 k = (z + d) % RING
-                for i, side in enumerate((1, -1)):
-                    g = (y_low + side + groups) % groups
-                    copy = remote(parts.at[g, k], ry.at[i, k], rys.at[i, d], ryr.at[i, k], at(y + side, z))
-                    copy.start()
-                    sent.append(copy)
+                side = jnp.where(k < far, 1, -1) * (-1 if relayed else 1)
+                i = (1 - side) // 2
+                g = (y_low + side + groups) % groups
+                if relayed:
+                    remote(rh.at[k], rh.at[k], rhs_.at[0], rhr.at[k], at(y, z + 1)).wait_recv()
+                    parts[g, k] = (parts[g, k].astype(f32) + rh[k].astype(f32)).astype(bf16)
+                copy = remote(
+                    parts.at[g, k], ry.at[i, k], rys.at[1 if relayed else 0, d], ryr.at[i, k],
+                    at(y + side, z),
+                )
+                copy.start()
+                sent.append(copy)
+
+            slots = far_first + [0]
+            for d in slots[:far]:
+                to_owner(d, False)
         weight_grads(y_low)
+        if groups == 4:
+            for i, d in enumerate(slots):
+                to_owner(d, True)
+                for later in slots[far + i : far + i + 1]:
+                    to_owner(later, False)
 
         def group_sum(k):
             total = parts[y_low, k].astype(f32)
             if groups == 4:
-                remote(rh.at[k], rh.at[k], rhs_.at[0], rhr.at[k], at(y, z + 1)).wait_recv()
                 for i in range(2):
                     remote(ry.at[i, k], ry.at[i, k], rys.at[i, 0], ryr.at[i, k], at(y, z + 1)).wait_recv()
-                total += ry[0, k].astype(f32) + ry[1, k].astype(f32) + rh[k].astype(f32)
+                total += ry[0, k].astype(f32) + ry[1, k].astype(f32)
             return total
 
         for d in far_first:

time: 104 us -> 102 us (0.981)
  the two profiles are of different devices: /device:TPU:8 before, /device:TPU:1 now
where the time goes in v4:
time: 102 us; the launch traced here: 101 us
  Pallas kernels  98.4 us (96%)
  local copies, waits for them, and re-layouts  1.51 us (1%)
    pallas_call x1, Pallas kernels, local(): pl.pallas_call(body, out_shape=jax.ShapeDtypeStruct((80, width), f32), in...  98.4 us

profile of v4, /device:TPU:1, one launch (start us, length us, event | category | flops | bytes accessed | tf_op | source)
XLA Modules:
  0.0 100.6 jit_solution(8945669283946898558)
XLA Ops:
  0.6 98.4 %shard_map.68 = f32[80,320]{1,0:T(8,128)} custom-call(bf16[4,320,128]{2,1,0:T(8,128)(2,1)} %bitcast.16, s32[4,128]{1,0:T(4,128)} %refs_1_.1, bf16[40,320]{1,0:T(8,128)(2,1)} %bitcast.17, bf16[40,320]{1,0:T(8,128)(2,1)} %bitcast.18, bf16[5,320]{1,0:T(8,128)(2,1)} %bitcast.19), custom_call_target="tpu_custom_call" | custom-call | tf_op jit(solution)/shard_map/pallas_call | solution.py:592
  99.1 1.5 %slice_bitcast_fusion = (f32[1,320,40]{1,2,0:T(8,128)}, f32[1,320,40]{1,2,0:T(8,128)}) fusion(f32[80,320]{1,0:T(8,128)} %shard_map.68), kind=kLoop, calls=%fused_computation | loop fusion | bytes 204800 | tf_op jit(solution)/shard_map/broadcast_in_dim | solution.py:655

commit v5 on v4

--- a/solution.py
+++ b/solution.py
@@ -249,11 +249,11 @@
                     forward_from(j, distance)
         for r in soon:
             unpack_column(r)
+        for copy in sent:
+            copy.wait_send()
         for j in order:
             arrived(slot(j, far))
         unpack_column(late)
-        for copy in sent:
-            copy.wait_send()
 
     near_first = [d for i in range(1, far) for d in (i, -i)] + [far]
 
@@ -284,6 +284,9 @@
                 arrived(index)
             sent += y_sends(index, len(sent))
         for r in soon + (late,):
+            if r == late:
+                for copy in sent:
+                    copy.wait_send()
             if groups == 4:
                 first = (z // 2 + r) % pairs * 2
                 for j in (1, 3, 2):
@@ -291,8 +294,6 @@
                         index += (y_low + j) % groups * RING
                         (halves_arrived if j == 2 else arrived)(index)
             unpack_column(r)
-        for copy in sent:
-            copy.wait_send()
 
     for copy in copies_in[2:]:
         copy.wait()
@@ -331,13 +332,15 @@
         nbuf[m] = normed
         low, high = normed[:256], low_pad(normed[256:])
         total = x.astype(f32)
+        active = []
         for first in range(0, hidden, fine):
             rows = slice(first, first + fine)
             before = nn(up_t[rows, :], low) + nn(mix_t[rows, :], high)
             pre[m, rows, :] = before
             bent = jnp.tanh(GELU_C * (before + GELU_A * (before * before * before)))
-            hid[m, rows, :] = (before * (0.5 * (1.0 + bent))).astype(bf16)
-        out = (total + nn(down_n[...], hid[m])).astype(bf16)
+            active.append((before * (0.5 * (1.0 + bent))).astype(bf16))
+            hid[m, rows, :] = active[-1]
+        out = (total + nn(down_n[...], jnp.concatenate(active, axis=0))).astype(bf16)
         obuf[m] = out
 
         @pl.when(s < last)
@@ -420,6 +423,17 @@
         both_out[40:80, 0:128] = result[80:120]
         both_out[40:80, 128:256] = result[120:160]
         both_out[40:80, 256:320] = result[160:200, 64:128]
+
+    def settle():
+        @pl.when(s < last)
+        def _():
+            for m in range(micro):
+                remote(obuf.at[m], xbuf.at[m], fs.at[m], fr.at[m], {"section": s + 1}).wait_send()
+
+        @pl.when(s > 0)
+        def _():
+            for m in range(micro):
+                remote(dsend.at[m], dybuf.at[m], bs.at[m], br.at[m], {"section": s - 1}).wait_send()
 
     @pl.when(sum_a)
     def _():
@@ -483,6 +497,9 @@
                     copy.start()
                     sent.append(copy)
         yall[y] = ysum[0]
+        settle()
+        for copy in sent:
+            copy.wait_send()
         for e in range(1, height):
             source = yall.at[(y + e) % height]
             remote(source, source, ys.at[0], yr.at[(y + e) % height], at(y, z + 1)).wait_recv()
@@ -490,8 +507,6 @@
         for e in range(1, height):
             total += yall[e].astype(f32)
         write(total)
-        for copy in sent:
-            copy.wait_send()
 
     @pl.when(jnp.logical_not(sum_a))
     def _():
@@ -551,6 +566,9 @@
             copy.start()
             sent.append(copy)
         result = group_sum(z)
+        settle()
+        for copy in sent:
+            copy.wait_send()
         for d in range(1, RING):
             remote(rz.at[d - 1], rz.at[d - 1], rzs.at[0], rzr.at[d - 1], at(y, z + 1)).wait_recv()
             result += rz[d - 1].astype(f32)
@@ -559,22 +577,9 @@
             tbuf[...] = rounded
             copy = remote(tbuf, rt, ts.at[0], tr.at[0], at(y + groups, z))
             copy.start()
-            sent.append(copy)
-            copy.wait_recv()
+            copy.wait()
             result = rounded.astype(f32) + rt[...].astype(f32)
         write(result)
-        for copy in sent:
-            copy.wait_send()
-
-    @pl.when(s < last)
-    def _():
-        for m in range(micro):
-            remote(obuf.at[m], xbuf.at[m], fs.at[m], fr.at[m], {"section": s + 1}).wait_send()
-
-    @pl.when(s > 0)
-    def _():
-        for m in range(micro):
-            remote(dsend.at[m], dybuf.at[m], bs.at[m], br.at[m], {"section": s - 1}).wait_send()
 
 
 def local(features, labels, w_expand, w_reduce, head_weight):

time: 102 us -> 102 us (level)
  the two profiles are of different devices: /device:TPU:1 before, /device:TPU:16 now
where the time goes in v5:
time: 102 us
  Pallas kernels  99.9 us (98%)
  local copies, waits for them, and re-layouts  1.51 us (1%)
    pallas_call x1, Pallas kernels, local(): pl.pallas_call(body, out_shape=jax.ShapeDtypeStruct((80, width), f32), in...  99.9 us

profile of v5, /device:TPU:16, one launch (start us, length us, event | category | flops | bytes accessed | tf_op | source)
XLA Modules:
  0.0 102.1 jit_solution(10702485686206175832)
XLA Ops:
  0.6 99.9 %shard_map.68 = f32[80,320]{1,0:T(8,128)} custom-call(bf16[4,320,128]{2,1,0:T(8,128)(2,1)} %bitcast.16, s32[4,128]{1,0:T(4,128)} %refs_1_.1, bf16[40,320]{1,0:T(8,128)(2,1)} %bitcast.17, bf16[40,320]{1,0:T(8,128)(2,1)} %bitcast.18, bf16[5,320]{1,0:T(8,128)(2,1)} %bitcast.19), custom_call_target="tpu_custom_call" | custom-call | tf_op jit(solution)/shard_map/pallas_call | solution.py:597
  100.6 1.5 %slice_bitcast_fusion = (f32[1,320,40]{1,2,0:T(8,128)}, f32[1,320,40]{1,2,0:T(8,128)}) fusion(f32[80,320]{1,0:T(8,128)} %shard_map.68), kind=kLoop, calls=%fused_computation | loop fusion | bytes 204800 | tf_op jit(solution)/shard_map/broadcast_in_dim | solution.py:660

commit v6 on v5

--- a/solution.py
+++ b/solution.py
@@ -198,11 +198,20 @@
     pairs = RING // 2
     soon, late = ((0, 1, 3), 2) if far == 4 else ((), 0)
 
+    def take_inputs():
+        for copy in copies_in[2:]:
+            copy.wait()
+
+        @pl.when(s == 0)
+        def _():
+            for m in range(micro):
+                xbuf[m] = feat[m]
+
     def unpack_column(r):
         def one(j, carry):
             return unpack((y_low + j) % groups * pairs + (z // 2 + r) % pairs, carry)
 
-        lax.fori_loop(0, groups, one, 0)
+        lax.fori_loop(0, groups, one, 0, unroll=r == late)
 
     @pl.when(is_a)
     def _():
@@ -249,6 +258,7 @@
                     forward_from(j, distance)
         for r in soon:
             unpack_column(r)
+        take_inputs()
         for copy in sent:
             copy.wait_send()
         for j in order:
@@ -285,6 +295,7 @@
             sent += y_sends(index, len(sent))
         for r in soon + (late,):
             if r == late:
+                take_inputs()
                 for copy in sent:
                     copy.wait_send()
             if groups == 4:
@@ -295,9 +306,6 @@
                         (halves_arrived if j == 2 else arrived)(index)
             unpack_column(r)
 
-    for copy in copies_in[2:]:
-        copy.wait()
-
     wide = eye(256)
     down_n[0:256, :] = nt(wide, down_t[...]).astype(bf16)
     turned = nt(eye(128), mix_t[...]).astype(bf16)
@@ -307,11 +315,6 @@
     def _():
         up_n[0:256, :] = nt(wide, up_t[...]).astype(bf16)
         up_n[256:320, :] = turned[0:64]
-
-    @pl.when(s == 0)
-    def _():
-        for m in range(micro):
-            xbuf[m] = feat[m]
 
     @pl.when(s == last)
     def _():

time: 102 us -> 101 us (level)
  the two profiles are of different devices: /device:TPU:16 before, /device:TPU:1 now
where the time goes in v6:
time: 101 us; the launch traced here: 100 us
  Pallas kernels  98 us (97%)
  local copies, waits for them, and re-layouts  1.51 us (1%)
    pallas_call x1, Pallas kernels, local(): pl.pallas_call(body, out_shape=jax.ShapeDtypeStruct((80, width), f32), in...  98 us

profile of v6, /device:TPU:1, one launch (start us, length us, event | category | flops | bytes accessed | tf_op | source)
XLA Modules:
  0.0 100.1 jit_solution(2000801710282127315)
XLA Ops:
  0.6 98.0 %shard_map.68 = f32[80,320]{1,0:T(8,128)} custom-call(bf16[4,320,128]{2,1,0:T(8,128)(2,1)} %bitcast.16, s32[4,128]{1,0:T(4,128)} %refs_1_.1, bf16[40,320]{1,0:T(8,128)(2,1)} %bitcast.17, bf16[40,320]{1,0:T(8,128)(2,1)} %bitcast.18, bf16[5,320]{1,0:T(8,128)(2,1)} %bitcast.19), custom_call_target="tpu_custom_call" | custom-call | tf_op jit(solution)/shard_map/pallas_call | solution.py:600
  98.6 1.5 %slice_bitcast_fusion = (f32[1,320,40]{1,2,0:T(8,128)}, f32[1,320,40]{1,2,0:T(8,128)}) fusion(f32[80,320]{1,0:T(8,128)} %shard_map.68), kind=kLoop, calls=%fused_computation | loop fusion | bytes 204800 | tf_op jit(solution)/shard_map/broadcast_in_dim | solution.py:663
